TPU v7x, 256 devices: a whole 4x4x8 slice. The times are simulated.
256 devices in a mesh: plane: 16 (over y, x_lo, core), across: 16 (over z, x_hi).
Axes of the slice: x: 4 (x_hi: 2, x_lo: 2; x = x_hi * 2 + x_lo), y: 4, z: 8, core: 2. Of those that a mesh axis runs over, the one named last changes fastest.
Arguments:
- labels: int32 [256, 1024, 1024], P('across', 'plane'), may hold values 0 or 1
- kappa: float32 [256, 1024, 1024], P('across', 'plane'), may hold values from 0.3 to 3
- inflow: float32 [1024, 1024], P('plane'), may hold values from 0.5 to 2
Outputs:
- level_new: float32 [256, 1024, 1024], P('across', 'plane')
- pressure: float32 [1024, 1024], P('plane', 'across')
All inputs are finite; a program needn't handle non-finite values. No bound on the sum of `labels` on one device may be relied on, other than what follows from the above.
Results may differ from a plain program's by a relative error of at most 0.000059.
Values sent between devices are 32-bit elements; how exact they have to be, the bound alone decides.
A program may use at most 64 MiB of HBM per device.

v0:
```python
import jax
import jax.numpy as jnp
from jax import lax
from jax.sharding import PartitionSpec as P

ITERS = 4


front_width = 0.5
time_step = 0.3
leak_rate = 0.05
cheb_low = 0.05
cheb_high = 2.0


def padded(cells, sides, width):
    for axis, dim in sides:
        count = lax.axis_size(axis)
        ends = count - 1
        head = lax.slice_in_dim(cells, 0, width, axis=dim)
        tail = lax.slice_in_dim(cells, cells.shape[dim] - width, cells.shape[dim], axis=dim)
        cells = jnp.concatenate(
            [
                lax.ppermute(tail, axis, [(i, (i + 1) % count) for i in range(ends)]),
                cells,
                lax.ppermute(head, axis, [((i + 1) % count, i) for i in range(ends)]),
            ],
            axis=dim,
        )
    return cells


def face_terms(padded_conduct):
    center = padded_conduct[1:-1, 1:-1]
    return (
        0.5 * (center + padded_conduct[2:, 1:-1]),
        0.5 * (center + padded_conduct[:-2, 1:-1]),
        0.5 * (center + padded_conduct[1:-1, 2:]),
        0.5 * (center + padded_conduct[1:-1, :-2]),
    )


def neighbour_sum(faces, padded_field):
    return (
        faces[0] * padded_field[2:, 1:-1]
        + faces[1] * padded_field[:-2, 1:-1]
        + faces[2] * padded_field[1:-1, 2:]
        + faces[3] * padded_field[1:-1, :-2]
    )


def chebyshev(faces, source, diagonal, padder):
    center = (cheb_high + cheb_low) / 2
    radius = (cheb_high - cheb_low) / 2
    sigma_ratio = center / radius
    rho_prev = 1.0 / sigma_ratio
    pressure = jnp.zeros_like(source)
    residue = source
    direction = source / (center * diagonal)
    for sweep_index in range(ITERS):
        pressure = pressure + direction
        if sweep_index < ITERS - 1:
            image = diagonal * direction - neighbour_sum(faces, padder(direction))
            residue = residue - image
            rho_next = 1.0 / (2 * sigma_ratio - rho_prev)
            direction = rho_next * rho_prev * direction + 2 * rho_next / radius * residue / diagonal
            rho_prev = rho_next
    return pressure


def rim_rows(field):
    extended = padded(field, (("plane", 0),), 1)
    return jnp.pad(extended, ((0, 0), (1, 1)))


def flux_field(conduct, pressure, padder):
    padded_press = padder(pressure)
    grad_x = 0.5 * (padded_press[2:, 1:-1] - padded_press[:-2, 1:-1])
    grad_y = 0.5 * (padded_press[1:-1, 2:] - padded_press[1:-1, :-2])
    return conduct * (grad_x * grad_x + grad_y * grad_y) + 0.05


def in_plane(aperture, react, inflow_part, padder):
    conduct = aperture**3 + 0.05
    row_count = aperture.shape[0]
    total_rows = row_count * lax.axis_size("plane")
    rows = (lax.axis_index("plane") * row_count + jnp.arange(row_count, dtype=jnp.int32)).astype(
        jnp.float32
    )
    ramp = 1.0 + 2.0 * rows / (total_rows - 1)
    source = ramp[:, None] * inflow_part + react
    faces = face_terms(padder(conduct))
    diagonal = faces[0] + faces[1] + faces[2] + faces[3] + leak_rate
    pressure = chebyshev(faces, source, diagonal, padder)
    return (pressure, flux_field(conduct, pressure, padder))


def column_parts(level, kappa, depth_total):
    tanh_level = jnp.tanh(level / front_width)
    aperture_part = jnp.sum(0.5 * (1.0 + tanh_level), axis=0) / depth_total
    react_part = jnp.sum(kappa * (1.0 - tanh_level * tanh_level), axis=0) / (
        2 * front_width * depth_total
    )
    return (aperture_part, react_part)


def on_device(labels, kappa, inflow):
    depth_total = labels.shape[0] * lax.axis_size("across")
    level = (1.0 - 2.0 * labels.astype(jnp.float32)) * kappa
    row_count, width = inflow.shape
    total_rows = row_count * lax.axis_size("plane")
    cell_total = total_rows * width
    tile_width = width // lax.axis_size("across")
    tile_start = lax.axis_index("across") * tile_width
    aperture_part, react_part = column_parts(level, kappa, depth_total)
    aperture, react = lax.psum((aperture_part, react_part), "across")
    pressure, flux = in_plane(aperture, react, inflow, rim_rows)
    flux_total = lax.psum(jnp.sum(flux), "plane")
    flux_norm = flux / (flux_total / cell_total)
    press_out = lax.dynamic_slice_in_dim(pressure, tile_start, tile_width, 1)
    padded_level = padded(level, (("plane", 1), ("across", 0)), 1)
    padded_level = jnp.pad(padded_level, ((0, 0), (0, 0), (1, 1)))
    grad_z = 0.5 * (padded_level[2:, 1:-1, 1:-1] - padded_level[:-2, 1:-1, 1:-1])
    grad_x = 0.5 * (padded_level[1:-1, 2:, 1:-1] - padded_level[1:-1, :-2, 1:-1])
    grad_y = 0.5 * (padded_level[1:-1, 1:-1, 2:] - padded_level[1:-1, 1:-1, :-2])
    slope = jnp.sqrt(grad_z * grad_z + grad_x * grad_x + grad_y * grad_y + 0.25)
    level_new = level + time_step * kappa * flux_norm[None] * slope
    return (level_new, press_out)


def solution(mesh):
    return jax.shard_map(
        on_device,
        mesh=mesh,
        in_specs=(P("across", "plane", None), P("across", "plane", None), P("plane", None)),
        out_specs=(P("across", "plane", None), P("plane", "across")),
        check_vma=False,
    )
```

profile of v0, /device:TPU:1, one launch (start us, length us, event | category | flops | bytes accessed | tf_op | source)
XLA Modules:
  0.0 290.1 jit_solution(9670967585383447386)
XLA Ops:
  7.2 0.0 all-reduce.9.cloned.1.call-start
  7.2 5.8 %multiply_reduce_fusion.1 = (f32[64,1024]{1,0:T(8,128)S(1)}, f32[64,1024]{1,0:T(8,128)S(1)}, f32[16,64,1024]{2,1,0:T(8,128)}) fusion(f32[16,64,1024]{2,1,0:T(8,128)} %param.4, s32[16,64,1024]{2,1,0:T(8,128)} %param.3), kind=kLoop, calls=%fused_computation.31 | loop fusion | flops 12451840 | bytes 13107200 | tf_op jit(solution)/shard_map/reduce_sum | solution.py:100
  13.0 0.8 broadcast_multiply_fusion
  13.8 0.0 all-reduce.9.cloned.1.call-update
  13.9 152.4 %all-reduce.9.cloned.1.call-done = (f32[64,1024]{1,0:T(8,128)}, f32[64,1024]{1,0:T(8,128)}) async-done(((f32[64,1024]{1,0:T(8,128)}, f32[64,1024]{1,0:T(8,128)}), (f32[64,1024]{1,0:T(8,128)}, f32[64,1024]{1,0:T(8,128)})) %all-reduce.9.cloned.1.call-update) | async-done | bytes 524304 | tf_op jit(solution)/shard_map/psum | solution.py:116
  166.2 1.0 fusion.16
  167.2 13.5 %collective-permute-start.1 = (f32[1,1024]{1,0:T(1,128)S(1)}, f32[1,1024]{1,0:T(1,128)S(1)}, u32[]{:S(2)}, u32[]{:S(2)}) collective-permute-start(f32[1,1024]{1,0:T(1,128)S(1)} %get-tuple-element.23), channel_id=1, source_target_pairs={{0,16},{16,32},{32,48},{48,64},{64,80},{80,96},{96,112},{112,128},... | collective-permute-start | bytes 12296 | tf_op jit(solution)/shard_map/ppermute | solution.py:24
  180.8 1.9 collective-permute-start
  182.7 0.0 collective-permute-done.1
  182.7 3.0 %collective-permute-done = f32[1,1024]{1,0:T(1,128)S(1)} collective-permute-done((f32[1,1024]{1,0:T(1,128)S(1)}, f32[1,1024]{1,0:T(1,128)S(1)}, u32[]{:S(2)}, u32[]{:S(2)}) %collective-permute-start) | collective-permute-done | bytes 4128 | tf_op jit(solution)/shard_map/ppermute | solution.py:26
  185.7 0.2 select_maximum_fusion.12
  185.9 1.2 multiply_divide_fusion
  187.1 1.9 collective-permute-start.3
  189.1 2.4 collective-permute-start.2
  191.4 1.3 fusion.58
  192.7 4.2 %collective-permute-start.10 = (f32[16,1,1024]{2,1,0:T(1,128)S(1)}, f32[16,1,1024]{2,1,0:T(1,128)S(1)}, u32[]{:S(2)}, u32[]{:S(2)}) collective-permute-start(f32[16,1,1024]{2,1,0:T(1,128)S(1)} %get-tuple-element.13), channel_id=1, source_target_pairs={{0,16},{16,32},{32,48},{48,64},{64,80},{80,96},{96,112},{112,128},... | collective-permute-start | bytes 196616 | tf_op jit(solution)/shard_map/ppermute | solution.py:24
  196.9 1.9 collective-permute-start.11
  198.8 0.0 collective-permute-done.3
  198.8 0.0 collective-permute-done.2
  198.9 0.2 select_maximum_fusion.10
  199.0 0.5 divide_add_fusion.1
  199.5 3.6 %collective-permute-start.5 = (f32[1,1024]{1,0:T(1,128)S(1)}, f32[1,1024]{1,0:T(1,128)S(1)}, u32[]{:S(2)}, u32[]{:S(2)}) collective-permute-start(f32[1,1024]{1,0:T(1,128)S(1)} %get-tuple-element.19), channel_id=1, source_target_pairs={{0,16},{16,32},{32,48},{48,64},{64,80},{80,96},{96,112},{112,128},... | collective-permute-start | bytes 12296 | tf_op jit(solution)/shard_map/ppermute | solution.py:24
  203.2 2.2 collective-permute-start.4
  205.4 0.0 collective-permute-done.10
  205.4 0.0 collective-permute-done.11
  205.4 1.1 pad_maximum_fusion.8
  206.5 4.3 %collective-permute-start.13 = (f32[1,66,1024]{2,1,0:T(8,128)S(1)}, f32[1,66,1024]{2,1,0:T(8,128)S(1)}, u32[]{:S(2)}, u32[]{:S(2)}) collective-permute-start(f32[1,66,1024]{2,1,0:T(8,128)S(1)} %get-tuple-element.11), channel_id=1, source_target_pairs={{0,1},{1,2},{2,3},{3,4},{4,5},{5,6},{6,7},{7,8},{8,9},{9,10},{10,1... | collective-permute-start | bytes 811016 | tf_op jit(solution)/shard_map/ppermute | solution.py:24
  210.8 1.3 collective-permute-start.12
  212.1 0.0 collective-permute-done.5
  212.1 0.0 collective-permute-done.4
  212.1 0.2 select_maximum_fusion.8
  212.3 0.7 divide_add_fusion
  213.1 3.3 %collective-permute-start.7 = (f32[1,1024]{1,0:T(1,128)S(1)}, f32[1,1024]{1,0:T(1,128)S(1)}, u32[]{:S(2)}, u32[]{:S(2)}) collective-permute-start(f32[1,1024]{1,0:T(1,128)S(1)} %get-tuple-element.17), channel_id=1, source_target_pairs={{0,16},{16,32},{32,48},{48,64},{64,80},{80,96},{96,112},{112,128},... | collective-permute-start | bytes 12296 | tf_op jit(solution)/shard_map/ppermute | solution.py:24
  216.4 1.9 collective-permute-start.6
  218.3 4.2 %collective-permute-done.13 = f32[1,66,1024]{2,1,0:T(8,128)S(1)} collective-permute-done((f32[1,66,1024]{2,1,0:T(8,128)S(1)}, f32[1,66,1024]{2,1,0:T(8,128)S(1)}, u32[]{:S(2)}, u32[]{:S(2)}) %collective-permute-start.13) | collective-permute-done | bytes 270368 | tf_op jit(solution)/shard_map/ppermute | solution.py:24
  222.5 0.0 collective-permute-done.12
  222.5 6.5 %select_maximum_fusion = f32[18,66,1026]{2,1,0:T(8,128)} fusion(f32[1,66,1024]{2,1,0:T(8,128)S(1)} %collective-permute-done.12, f32[1,66,1024]{2,1,0:T(8,128)S(1)} %collective-permute-done.13, f32[16,1,1024]{2,1,0:T(1,128)S(1)} %collective-permute-done.11, f32[16,64,1024]{2,1,0:T(8,128)S(1)} %copy-done, f32[16,1,1024]{2,1,0:T(1,128)S(1)} %collective-permute-done.10), kind=kLoop, calls=%fused_computation.2 | loop fusion | flops 14626656 | bytes 9741600 | tf_op jit(solution)/shard_map/concatenate | solution.py:22
  229.0 0.2 select_maximum_fusion.6
  229.2 1.1 fusion.31
  230.3 4.3 %collective-permute-start.9 = (f32[1,1024]{1,0:T(1,128)S(1)}, f32[1,1024]{1,0:T(1,128)S(1)}, u32[]{:S(2)}, u32[]{:S(2)}) collective-permute-start(f32[1,1024]{1,0:T(1,128)S(1)} %get-tuple-element.15), channel_id=1, source_target_pairs={{0,16},{16,32},{32,48},{48,64},{64,80},{80,96},{96,112},{112,128},... | collective-permute-start | bytes 12296 | tf_op jit(solution)/shard_map/ppermute | solution.py:24
  234.6 1.9 collective-permute-start.8
  236.5 0.7 constant_dynamic-slice_fusion
  237.2 0.0 collective-permute-done.9
  237.2 2.3 collective-permute-done.8
  239.5 0.2 select_maximum_fusion.4
  239.7 0.8 fusion.56
  240.5 25.4 %psum.23 = f32[]{:T(128)} all-reduce(f32[]{:T(128)} %get-tuple-element.6), channel_id=1, replica_groups=mesh['plane'=16,'across'=16] {'plane'}, use_global_device_ids=true, to_apply=%region_5.6 | all-reduce | flops 1 | bytes 8 | tf_op jit(solution)/shard_map/psum | solution.py:118
  266.6 16.6 %fusion.7 = f32[16,64,1024]{2,1,0:T(8,128)} fusion(f32[16,64,1024]{2,1,0:T(8,128)} %get-tuple-element.10, f32[18,66,1026]{2,1,0:T(8,128)} %select_maximum_fusion, f32[16,1,1024]{2,1,0:T(1,128)S(1)} %collective-permute-done.10, f32[16,1,1024]{2,1,0:T(1,128)S(1)} %collective-permute-done.11, f32[1,66,1024]{2,1,0:T(8,128)S(1)} %collective-permute-done.13, ...), kind=kLoop, calls=%fused_computation.14 | loop fusion | flops 24117248 | bytes 21905408 | tf_op jit(solution)/shard_map/add | solution.py:127
  (15 shorter events, 0.1 us)
Async XLA Ops:
  7.2 178.7 %copy-start.2 = (f32[64,1024]{1,0:T(8,128)S(1)}, f32[64,1024]{1,0:T(8,128)}, u32[]{:S(2)}) copy-start(f32[64,1024]{1,0:T(8,128)} %param.5) | copy-start | bytes 786436
  7.2 159.0 %all-reduce.9.cloned.1.call-start = ((), (), s32[]{:S(2)}) async-start(), calls=%async_computation | async-start | bytes 1048576 | tf_op jit(solution)/shard_map/psum | solution.py:116
  167.2 15.5 %collective-permute-start.1 = (f32[1,1024]{1,0:T(1,128)S(1)}, f32[1,1024]{1,0:T(1,128)S(1)}, u32[]{:S(2)}, u32[]{:S(2)}) collective-permute-start(f32[1,1024]{1,0:T(1,128)S(1)} %get-tuple-element.23), channel_id=1, source_target_pairs={{0,16},{16,32},{32,48},{48,64},{64,80},{80,96},{96,112},{112,128},... | collective-permute-start | bytes 12296 | tf_op jit(solution)/shard_map/ppermute | solution.py:24
  180.8 4.9 %collective-permute-start = (f32[1,1024]{1,0:T(1,128)S(1)}, f32[1,1024]{1,0:T(1,128)S(1)}, u32[]{:S(2)}, u32[]{:S(2)}) collective-permute-start(f32[1,1024]{1,0:T(1,128)S(1)} %get-tuple-element.24), channel_id=1, source_target_pairs={{16,0},{32,16},{48,32},{64,48},{80,64},{96,80},{112,96},{128,112},... | collective-permute-start | bytes 12296 | tf_op jit(solution)/shard_map/ppermute | solution.py:26
  187.1 11.7 %collective-permute-start.3 = (f32[1,1024]{1,0:T(1,128)S(1)}, f32[1,1024]{1,0:T(1,128)S(1)}, u32[]{:S(2)}, u32[]{:S(2)}) collective-permute-start(f32[1,1024]{1,0:T(1,128)S(1)} %get-tuple-element.21), channel_id=1, source_target_pairs={{0,16},{16,32},{32,48},{48,64},{64,80},{80,96},{96,112},{112,128},... | collective-permute-start | bytes 12296 | tf_op jit(solution)/shard_map/ppermute | solution.py:24
  189.1 9.8 %collective-permute-start.2 = (f32[1,1024]{1,0:T(1,128)S(1)}, f32[1,1024]{1,0:T(1,128)S(1)}, u32[]{:S(2)}, u32[]{:S(2)}) collective-permute-start(f32[1,1024]{1,0:T(1,128)S(1)} %get-tuple-element.22), channel_id=1, source_target_pairs={{16,0},{32,16},{48,32},{64,48},{80,64},{96,80},{112,96},{128,112},... | collective-permute-start | bytes 12296 | tf_op jit(solution)/shard_map/ppermute | solution.py:26
  192.7 12.7 %collective-permute-start.10 = (f32[16,1,1024]{2,1,0:T(1,128)S(1)}, f32[16,1,1024]{2,1,0:T(1,128)S(1)}, u32[]{:S(2)}, u32[]{:S(2)}) collective-permute-start(f32[16,1,1024]{2,1,0:T(1,128)S(1)} %get-tuple-element.13), channel_id=1, source_target_pairs={{0,16},{16,32},{32,48},{48,64},{64,80},{80,96},{96,112},{112,128},... | collective-permute-start | bytes 196616 | tf_op jit(solution)/shard_map/ppermute | solution.py:24
  196.9 8.5 %collective-permute-start.11 = (f32[16,1,1024]{2,1,0:T(1,128)S(1)}, f32[16,1,1024]{2,1,0:T(1,128)S(1)}, u32[]{:S(2)}, u32[]{:S(2)}) collective-permute-start(f32[16,1,1024]{2,1,0:T(1,128)S(1)} %get-tuple-element.14), channel_id=1, source_target_pairs={{16,0},{32,16},{48,32},{64,48},{80,64},{96,80},{112,96},{128,112},... | collective-permute-start | bytes 196616 | tf_op jit(solution)/shard_map/ppermute | solution.py:26
  199.5 12.6 %collective-permute-start.5 = (f32[1,1024]{1,0:T(1,128)S(1)}, f32[1,1024]{1,0:T(1,128)S(1)}, u32[]{:S(2)}, u32[]{:S(2)}) collective-permute-start(f32[1,1024]{1,0:T(1,128)S(1)} %get-tuple-element.19), channel_id=1, source_target_pairs={{0,16},{16,32},{32,48},{48,64},{64,80},{80,96},{96,112},{112,128},... | collective-permute-start | bytes 12296 | tf_op jit(solution)/shard_map/ppermute | solution.py:24
  203.2 19.3 %copy-start = (f32[16,64,1024]{2,1,0:T(8,128)S(1)}, f32[16,64,1024]{2,1,0:T(8,128)}, u32[]{:S(2)}) copy-start(f32[16,64,1024]{2,1,0:T(8,128)} %get-tuple-element.10) | copy-start | bytes 12582916
  203.2 8.9 %collective-permute-start.4 = (f32[1,1024]{1,0:T(1,128)S(1)}, f32[1,1024]{1,0:T(1,128)S(1)}, u32[]{:S(2)}, u32[]{:S(2)}) collective-permute-start(f32[1,1024]{1,0:T(1,128)S(1)} %get-tuple-element.20), channel_id=1, source_target_pairs={{16,0},{32,16},{48,32},{64,48},{80,64},{96,80},{112,96},{128,112},... | collective-permute-start | bytes 12296 | tf_op jit(solution)/shard_map/ppermute | solution.py:26
  206.5 16.0 %collective-permute-start.13 = (f32[1,66,1024]{2,1,0:T(8,128)S(1)}, f32[1,66,1024]{2,1,0:T(8,128)S(1)}, u32[]{:S(2)}, u32[]{:S(2)}) collective-permute-start(f32[1,66,1024]{2,1,0:T(8,128)S(1)} %get-tuple-element.11), channel_id=1, source_target_pairs={{0,1},{1,2},{2,3},{3,4},{4,5},{5,6},{6,7},{7,8},{8,9},{9,10},{10,1... | collective-permute-start | bytes 811016 | tf_op jit(solution)/shard_map/ppermute | solution.py:24
  210.8 11.7 %collective-permute-start.12 = (f32[1,66,1024]{2,1,0:T(8,128)S(1)}, f32[1,66,1024]{2,1,0:T(8,128)S(1)}, u32[]{:S(2)}, u32[]{:S(2)}) collective-permute-start(f32[1,66,1024]{2,1,0:T(8,128)S(1)} %get-tuple-element.12), channel_id=1, source_target_pairs={{1,0},{2,1},{3,2},{4,3},{5,4},{6,5},{7,6},{8,7},{9,8},{10,9},{11,1... | collective-permute-start | bytes 811016 | tf_op jit(solution)/shard_map/ppermute | solution.py:26
  213.1 15.9 %collective-permute-start.7 = (f32[1,1024]{1,0:T(1,128)S(1)}, f32[1,1024]{1,0:T(1,128)S(1)}, u32[]{:S(2)}, u32[]{:S(2)}) collective-permute-start(f32[1,1024]{1,0:T(1,128)S(1)} %get-tuple-element.17), channel_id=1, source_target_pairs={{0,16},{16,32},{32,48},{48,64},{64,80},{80,96},{96,112},{112,128},... | collective-permute-start | bytes 12296 | tf_op jit(solution)/shard_map/ppermute | solution.py:24
  216.4 12.6 %collective-permute-start.6 = (f32[1,1024]{1,0:T(1,128)S(1)}, f32[1,1024]{1,0:T(1,128)S(1)}, u32[]{:S(2)}, u32[]{:S(2)}) collective-permute-start(f32[1,1024]{1,0:T(1,128)S(1)} %get-tuple-element.18), channel_id=1, source_target_pairs={{16,0},{32,16},{48,32},{64,48},{80,64},{96,80},{112,96},{128,112},... | collective-permute-start | bytes 12296 | tf_op jit(solution)/shard_map/ppermute | solution.py:26
  229.0 10.7 %copy-start.1 = (f32[64,1024]{1,0:T(8,128)S(1)}, f32[64,1024]{1,0:T(8,128)}, u32[]{:S(2)}) copy-start(f32[64,1024]{1,0:T(8,128)} %get-tuple-element.5) | copy-start | bytes 786436
  230.3 7.0 %collective-permute-start.9 = (f32[1,1024]{1,0:T(1,128)S(1)}, f32[1,1024]{1,0:T(1,128)S(1)}, u32[]{:S(2)}, u32[]{:S(2)}) collective-permute-start(f32[1,1024]{1,0:T(1,128)S(1)} %get-tuple-element.15), channel_id=1, source_target_pairs={{0,16},{16,32},{32,48},{48,64},{64,80},{80,96},{96,112},{112,128},... | collective-permute-start | bytes 12296 | tf_op jit(solution)/shard_map/ppermute | solution.py:24
  234.6 4.9 %collective-permute-start.8 = (f32[1,1024]{1,0:T(1,128)S(1)}, f32[1,1024]{1,0:T(1,128)S(1)}, u32[]{:S(2)}, u32[]{:S(2)}) collective-permute-start(f32[1,1024]{1,0:T(1,128)S(1)} %get-tuple-element.16), channel_id=1, source_target_pairs={{16,0},{32,16},{48,32},{64,48},{80,64},{96,80},{112,96},{128,112},... | collective-permute-start | bytes 12296 | tf_op jit(solution)/shard_map/ppermute | solution.py:26
Sparse Core Ops, SparseCore 0:
  14.0 152.1 all-reduce.8
where the time goes:
time: 295 us; the launch traced here: 290 us
  waiting for transfers between devices  162 us (55%)
  starting transfers between devices  48.8 us (17%)
  other arithmetic  36.9 us (13%)
  blocking collectives  25.4 us (9%)
  between operations  15 us (5%)
    psum x1, waiting for transfers between devices, on_device(): aperture, react = lax.psum((aperture_part, react_part), 'across')  152 us
    ppermute x7, starting transfers between devices, padded(): lax.ppermute(tail, axis, [(i, (i + 1) % count) for i in range(ends)])  35.3 us
    psum x1, blocking collectives, on_device(): flux_total = lax.psum(jnp.sum(flux), 'plane')  25.4 us
    add x1, other arithmetic, on_device(): level_new = level + time_step * kappa * flux_norm[None] * slope  16.6 us
    ppermute x7, starting transfers between devices, padded(): lax.ppermute(head, axis, [((i + 1) % count, i) for i in range(ends)])  13.5 us
    concatenate x7, other arithmetic, padded(): jnp.concatenate([lax.ppermute(tail, axis, [(i, (i + 1) % count) for i in...  8.41 us
  transfers between devices with their start and end apart: 15, of which 4 were waited for; matrix products, arithmetic and copies ran while one was open for 4% of the time, Pallas kernels for 0%

commit v1 on v0

v1 whole, which is shorter than its diff:
```python
import functools

import jax
import jax.numpy as jnp
from jax import lax
from jax.experimental import pallas as pl
from jax.experimental.pallas import tpu as pltpu
from jax.sharding import PartitionSpec as P

ITERS = 4

front_width = 0.5
time_step = 0.3
leak_rate = 0.05
cheb_low = 0.05
cheb_high = 2.0

MESH = pl.DeviceIdType.MESH
F32 = jnp.float32

DEPTH = 16
ROWS = 64
WIDTH = 1024
GROUP = 16
LINES = 8
BLOCKS = ROWS // LINES
HALF = WIDTH // 2
STRIP = 128
RING = HALF + STRIP
PAD = 8
CELLS = float(ROWS * GROUP * WIDTH)
VOXELS = float(DEPTH * GROUP)
TOP_ROW = ROWS * GROUP - 1


def far_first(c):
    return 4 + (1 - 2 * lax.rem(c, 2)) * ((c + 1) // 2)


def near_first(c):
    return lax.rem(GROUP + (2 * lax.rem(c, 2) - 1) * ((c + 1) // 2), GROUP)


def aligned(index, step):
    return pl.ds(pl.multiple_of(index * step, step), step)


def kernel(
    labels, kappa, inflow, out, press_out,
    lab, kap, lev, flow, part, got, mine, gathered, rim, rim_got,
    tile, strip, up, down, strip_mid, strip_up, strip_down,
    sums, sums_plane, fluxes, press, press_got,
    lab_sem, kap_sem, flow_sem, xs_sem, xr_sem, zs_sem, zr_sem, hs_sem, hr_sem,
    as_sem, ar_sem, ps_sem, pr_sem, fs_sem, fr_sem, ts_sem, tr_sem, ls_sem, lr_sem, rs_sem, rr_sem,
):
    a = lax.axis_index("across")
    p = lax.axis_index("plane")
    z = a // 2
    xh = lax.rem(a, 2)
    other = 1 - xh
    partner = a + other - xh

    def on_across(index):
        return {"plane": p, "across": index}

    def on_plane(index):
        return {"plane": index, "across": a}

    def ring(index, step):
        return lax.rem(index + step + GROUP, GROUP)

    block_id = p * BLOCKS + z
    count = GROUP * BLOCKS
    before = lax.rem(block_id + count - 1, count)
    after = lax.rem(block_id + 1, count)

    def owner(block, side):
        return {"plane": block // BLOCKS, "across": 2 * lax.rem(block, BLOCKS) + side}

    def send(src, dst, send_sem, recv_sem, device):
        return pltpu.make_async_remote_copy(
            src_ref=src, dst_ref=dst, send_sem=send_sem, recv_sem=recv_sem,
            device_id=device, device_id_type=MESH,
        )

    def block_at(c):
        return lax.rem(z + far_first(c), BLOCKS)

    def load_labels(c):
        rows = aligned(block_at(c), LINES)
        return pltpu.make_async_copy(labels.at[:, rows, :], lab.at[:, rows, :], lab_sem.at[c])

    def load_kappa(c):
        rows = aligned(block_at(c), LINES)
        return pltpu.make_async_copy(kappa.at[:, rows, :], kap.at[:, rows, :], kap_sem.at[c])

    @pl.loop(0, BLOCKS)
    def _(c):
        load_labels(c).start()
        load_kappa(c).start()

    my_rows = aligned(z, LINES)
    my_columns = aligned(xh, HALF)
    load_flow = pltpu.make_async_copy(inflow.at[my_rows, my_columns], flow, flow_sem)
    load_flow.start()

    barrier = pltpu.get_barrier_semaphore()

    @pl.loop(1, GROUP)
    def _(k):
        pl.semaphore_signal(barrier, inc=1, device_id=on_across(ring(a, k)), device_id_type=MESH)
        pl.semaphore_signal(barrier, inc=1, device_id=on_plane(ring(p, k)), device_id_type=MESH)

    for block in (before, after):
        for side in (xh, other):
            pl.semaphore_signal(barrier, inc=1, device_id=owner(block, side), device_id_type=MESH)

    def column_sums(c):
        block = block_at(c)
        rows = aligned(block, LINES)
        load_labels(c).wait()
        load_kappa(c).wait()
        open_sum = jnp.zeros((LINES, WIDTH), F32)
        react_sum = jnp.zeros((LINES, WIDTH), F32)
        for k in range(DEPTH):
            rate = kap[k, rows, :]
            level = jnp.where(lab[k, rows, :] == 0, rate, -rate)
            lev[k + 1, pl.ds(pl.multiple_of(block * LINES + PAD, LINES), LINES), :] = level
            front = jnp.tanh(level * (1.0 / front_width))
            open_sum = open_sum + front
            react_sum = react_sum + rate * (1.0 - front * front)
        for side in range(2):
            part[side, block, 0] = open_sum[:, side * HALF : (side + 1) * HALF]
            part[side, block, 1] = react_sum[:, side * HALF : (side + 1) * HALF]

    def to_partner(c):
        block = block_at(c)
        return send(part.at[other, block], got.at[c], xs_sem.at[c], xr_sem.at[c], on_across(partner))

    early = 4

    @pl.loop(0, early)
    def _(c):
        column_sums(c)

    pl.semaphore_wait(barrier, 2 * (GROUP - 1) + 4)

    @pl.loop(0, early)
    def _(c):
        to_partner(c).start()

    @pl.loop(early, BLOCKS)
    def _(c):
        column_sums(c)
        to_partner(c).start()

    for k in range(DEPTH):
        rim[0, k : k + 1, :] = lev[k + 1, PAD : PAD + 1, :]
        rim[1, k : k + 1, :] = lev[k + 1, PAD + ROWS - 1 : PAD + ROWS, :]
    rims = [
        send(rim.at[0], rim_got.at[1], rs_sem.at[0], rr_sem.at[0], on_plane(ring(p, -1))),
        send(rim.at[1], rim_got.at[0], rs_sem.at[1], rr_sem.at[1], on_plane(ring(p, 1))),
    ]
    for copy in rims:
        copy.start()

    def to_owner(c):
        return send(
            mine.at[c], gathered.at[c], zs_sem.at[c], zr_sem.at[c],
            on_across(2 * block_at(c) + xh),
        )

    @pl.loop(0, BLOCKS - 1)
    def _(c):
        to_partner(c).wait_recv()
        mine[c] = part[xh, block_at(c)] + got[c]
        to_owner(c).start()

    to_partner(BLOCKS - 1).wait_recv()
    mine[BLOCKS - 1] = part[xh, z] + got[BLOCKS - 1]

    body = pl.ds(PAD, ROWS)
    layers = [
        send(lev.at[1, body, :], lev.at[DEPTH + 1, body, :], ls_sem.at[0], lr_sem.at[0], on_across(ring(a, -1))),
        send(lev.at[DEPTH, body, :], lev.at[0, body, :], ls_sem.at[1], lr_sem.at[1], on_across(ring(a, 1))),
    ]
    for copy in layers:
        copy.start()

    for copy in rims:
        copy.wait_recv()
    for k in range(DEPTH):
        lev[k + 1, PAD - 1 : PAD, :] = jnp.where(p == 0, 0.0, rim_got[0, k : k + 1, :])
        lev[k + 1, PAD + ROWS : PAD + ROWS + 1, :] = jnp.where(p == GROUP - 1, 0.0, rim_got[1, k : k + 1, :])

    lane = lax.broadcasted_iota(jnp.int32, (LINES, WIDTH), 1)

    def growth(k):
        for block in range(BLOCKS):
            first = PAD + block * LINES
            here = lev[k + 1, first : first + LINES, :]
            dz = lev[k + 2, first : first + LINES, :] - lev[k, first : first + LINES, :]
            dx = lev[k + 1, first + 1 : first + LINES + 1, :] - lev[k + 1, first - 1 : first + LINES - 1, :]
            right = jnp.where(lane == WIDTH - 1, 0.0, pltpu.roll(here, WIDTH - 1, 1))
            left = jnp.where(lane == 0, 0.0, pltpu.roll(here, 1, 1))
            dy = right - left
            slope = jnp.sqrt(dz * dz + dx * dx + dy * dy + 1.0)
            kap[k, block * LINES : (block + 1) * LINES, :] = (0.5 * time_step) * jnp.abs(here) * slope

    @pl.loop(1, DEPTH - 1)
    def _(k):
        growth(k)

    open_sum = mine[BLOCKS - 1, 0]
    react_sum = mine[BLOCKS - 1, 1]
    for c in range(BLOCKS - 1):
        to_owner(c).wait_recv()
        open_sum = open_sum + gathered[c, 0]
        react_sum = react_sum + gathered[c, 1]
    aperture = 0.5 + open_sum * (0.5 / VOXELS)
    react = react_sum * (1.0 / (2 * front_width * VOXELS))
    load_flow.wait()
    row = (block_id * LINES + lax.broadcasted_iota(jnp.int32, (LINES, HALF), 0)).astype(F32)
    tile[0] = aperture * aperture * aperture + 0.05
    tile[1] = (1.0 + 2.0 * row / TOP_ROW) * flow[...] + react
    strip[...] = tile[:, :, pl.ds(pl.multiple_of(other * (HALF - STRIP), STRIP), STRIP)]

    rims_of_tile = [
        send(tile, down, hs_sem.at[0], hr_sem.at[0], owner(before, xh)),
        send(tile, up, hs_sem.at[1], hr_sem.at[1], owner(after, xh)),
        send(strip, strip_down, hs_sem.at[2], hr_sem.at[2], owner(before, other)),
        send(strip, strip_up, hs_sem.at[3], hr_sem.at[3], owner(after, other)),
        send(strip, strip_mid, hs_sem.at[4], hr_sem.at[4], on_across(partner)),
    ]
    for copy in rims_of_tile:
        copy.start()
    for copy in rims_of_tile:
        copy.wait_recv()

    at_top = block_id == 0
    at_foot = block_id == count - 1

    def around(f):
        above = jnp.concatenate([up[f], strip_up[f]], axis=1)
        level_with = jnp.concatenate([tile[f], strip_mid[f]], axis=1)
        below = jnp.concatenate([down[f], strip_down[f]], axis=1)
        return jnp.concatenate(
            [jnp.where(at_top, 0.0, above), level_with, jnp.where(at_foot, 0.0, below)], axis=0
        )

    shape = (3 * LINES, RING)
    row_at = (block_id - 1) * LINES + lax.broadcasted_iota(jnp.int32, shape, 0)
    column_at = lax.broadcasted_iota(jnp.int32, shape, 1)
    has_up = row_at != 0
    has_down = row_at != TOP_ROW
    has_left = column_at != xh * HALF
    has_right = column_at != RING - 1 - xh * STRIP

    def from_up(v):
        return pltpu.roll(v, 1, 0)

    def from_down(v):
        return pltpu.roll(v, 3 * LINES - 1, 0)

    def from_left(v):
        return pltpu.roll(v, 1, 1)

    def from_right(v):
        return pltpu.roll(v, RING - 1, 1)

    sides = ((from_down, has_down), (from_up, has_up), (from_right, has_right), (from_left, has_left))
    conduct = around(0)
    residue = around(1)
    diagonal = jnp.full(shape, leak_rate, F32)
    weights = []
    for shift, inside in sides:
        face = 0.5 * (conduct + jnp.where(inside, shift(conduct), 0.0))
        diagonal = diagonal + face
        weights.append(jnp.where(inside, face, 0.0))
    inverse = 1.0 / diagonal
    center = (cheb_high + cheb_low) / 2
    radius = (cheb_high - cheb_low) / 2
    sigma_ratio = center / radius
    rho_prev = 1.0 / sigma_ratio
    pressure = jnp.zeros(shape, F32)
    direction = residue * inverse * (1.0 / center)
    for sweep_index in range(ITERS):
        pressure = pressure + direction
        if sweep_index < ITERS - 1:
            image = diagonal * direction
            for weight, (shift, _) in zip(weights, sides):
                image = image - weight * shift(direction)
            residue = residue - image
            rho_next = 1.0 / (2 * sigma_ratio - rho_prev)
            direction = rho_next * rho_prev * direction + (2 * rho_next / radius) * (residue * inverse)
            rho_prev = rho_next
    grad = []
    for shift, inside in sides:
        grad.append(jnp.where(inside, shift(pressure), 0.0))
    grad_x = 0.5 * (grad[0] - grad[1])
    grad_y = 0.5 * (grad[2] - grad[3])
    flux = (conduct * (grad_x * grad_x + grad_y * grad_y) + 0.05)[LINES : 2 * LINES, :HALF]
    fluxes[0] = flux
    total = flux[:, 0:STRIP]
    for c in range(1, HALF // STRIP):
        total = total + flux[:, c * STRIP : (c + 1) * STRIP]
    sums[0] = total
    for c in range(HALF // STRIP):
        press[c] = pressure[LINES : 2 * LINES, c * STRIP : (c + 1) * STRIP]

    def sum_across(k):
        return send(sums.at[0], sums.at[k], as_sem.at[k], ar_sem.at[k], on_across(ring(a, k)))

    def sum_plane(k):
        return send(sums_plane.at[0], sums_plane.at[k], ps_sem.at[k], pr_sem.at[k], on_plane(ring(p, k)))

    def flux_across(k):
        return send(fluxes.at[0], fluxes.at[k], fs_sem.at[k], fr_sem.at[k], on_across(ring(a, k)))

    @pl.loop(0, GROUP - 1)
    def _(c):
        sum_across(near_first(GROUP - 1 - c)).start()

    @pl.loop(0, GROUP - 1)
    def _(c):
        flux_across(near_first(GROUP - 1 - c)).start()

    def to_columns(j):
        return send(press.at[j // 2], press_got.at[z], ts_sem.at[j], tr_sem.at[z], on_across(BLOCKS * xh + j))

    @pl.loop(0, BLOCKS)
    def _(j):
        @pl.when(BLOCKS * xh + j != a)
        def _():
            to_columns(j).start()

        @pl.when(BLOCKS * xh + j == a)
        def _():
            press_got[z] = press[j // 2]

    @pl.loop(1, GROUP)
    def _(k):
        sum_across(k).wait_recv()

    total = sums[0]
    for k in range(1, GROUP):
        total = total + sums[k]
    sums_plane[0] = total

    @pl.loop(1, GROUP)
    def _(k):
        sum_plane(k).start()

    for copy in layers:
        copy.wait_recv()

    @pl.when(a == 0)
    def _():
        lev[0, PAD : PAD + ROWS, :] = jnp.zeros((ROWS, WIDTH), F32)

    @pl.when(a == GROUP - 1)
    def _():
        lev[DEPTH + 1, PAD : PAD + ROWS, :] = jnp.zeros((ROWS, WIDTH), F32)

    growth(0)
    growth(DEPTH - 1)

    @pl.loop(1, GROUP)
    def _(k):
        sum_plane(k).wait_recv()

    total = sums_plane[0]
    for k in range(1, GROUP):
        total = total + sums_plane[k]
    scale = CELLS / jnp.sum(jnp.sum(total, axis=0, keepdims=True), axis=1, keepdims=True)

    def advance(k):
        source = ring(a, -k)
        rows = aligned(source // 2, LINES)
        rows_lev = pl.ds(pl.multiple_of((source // 2) * LINES + PAD, LINES), LINES)
        columns = aligned(lax.rem(source, 2), HALF)
        norm = fluxes[k] * scale
        for layer in range(DEPTH):
            out[layer, rows, columns] = lev[layer + 1, rows_lev, columns] + kap[layer, rows, columns] * norm

    advance(0)

    @pl.loop(1, GROUP)
    def _(c):
        k = near_first(c)
        flux_across(k).wait_recv()
        advance(k)

    @pl.loop(0, BLOCKS)
    def _(source):
        @pl.when(2 * source + a // BLOCKS != a)
        def _():
            send(
                press.at[0], press_got.at[source], ts_sem.at[0], tr_sem.at[source],
                on_across(ring(2 * source + a // BLOCKS, 0)),
            ).wait_recv()

    for block in range(BLOCKS):
        piece = press_got[block]
        piece = jnp.where(xh == 1, pltpu.roll(piece, STRIP // 2, 1), piece)
        press_out[block * LINES : (block + 1) * LINES, :] = piece[:, : STRIP // 2]

    @pl.loop(0, BLOCKS)
    def _(c):
        to_partner(c).wait_send()

    @pl.loop(0, BLOCKS - 1)
    def _(c):
        to_owner(c).wait_send()

    for copy in rims + layers + rims_of_tile:
        copy.wait_send()

    @pl.loop(1, GROUP)
    def _(k):
        sum_across(k).wait_send()
        sum_plane(k).wait_send()
        flux_across(k).wait_send()

    @pl.loop(0, BLOCKS)
    def _(j):
        @pl.when(BLOCKS * xh + j != a)
        def _():
            to_columns(j).wait_send()


def on_device(labels, kappa, inflow):
    vmem = functools.partial(pltpu.VMEM, dtype=F32)
    dma = lambda n: pltpu.SemaphoreType.DMA((n,))
    hbm = pl.BlockSpec(memory_space=pltpu.HBM)
    whole = pl.BlockSpec(memory_space=pltpu.VMEM)
    labels, kappa, inflow = (pltpu.with_memory_space_constraint(x, pltpu.HBM) for x in (labels, kappa, inflow))
    return pl.pallas_call(
        kernel,
        out_shape=(
            jax.ShapeDtypeStruct((DEPTH, ROWS, WIDTH), F32),
            jax.ShapeDtypeStruct((ROWS, STRIP // 2), F32),
        ),
        in_specs=[hbm, hbm, hbm],
        out_specs=(whole, whole),
        scratch_shapes=[
            pltpu.VMEM((DEPTH, ROWS, WIDTH), jnp.int32),
            vmem((DEPTH, ROWS, WIDTH)),
            vmem((DEPTH + 2, ROWS + 2 * PAD, WIDTH)),
            vmem((LINES, HALF)),
            vmem((2, BLOCKS, 2, LINES, HALF)),
            vmem((BLOCKS, 2, LINES, HALF)),
            vmem((BLOCKS, 2, LINES, HALF)),
            vmem((BLOCKS, 2, LINES, HALF)),
            vmem((2, DEPTH, WIDTH)),
            vmem((2, DEPTH, WIDTH)),
            vmem((2, LINES, HALF)),
            vmem((2, LINES, STRIP)),
            vmem((2, LINES, HALF)),
            vmem((2, LINES, HALF)),
            vmem((2, LINES, STRIP)),
            vmem((2, LINES, STRIP)),
            vmem((2, LINES, STRIP)),
            vmem((GROUP, LINES, STRIP)),
            vmem((GROUP, LINES, STRIP)),
            vmem((GROUP, LINES, HALF)),
            vmem((HALF // STRIP, LINES, STRIP)),
            vmem((BLOCKS, LINES, STRIP)),
            dma(BLOCKS), dma(BLOCKS), pltpu.SemaphoreType.DMA,
            dma(BLOCKS), dma(BLOCKS),
            dma(BLOCKS), dma(BLOCKS),
            dma(5), dma(5),
            dma(GROUP), dma(GROUP), dma(GROUP), dma(GROUP),
            dma(GROUP), dma(GROUP),
            dma(BLOCKS), dma(BLOCKS),
            dma(2), dma(2), dma(2), dma(2),
        ],
        compiler_params=pltpu.CompilerParams(
            collective_id=0, has_side_effects=True, vmem_limit_bytes=40 * 2**20
        ),
        cost_estimate=pl.CostEstimate(
            flops=60 * DEPTH * ROWS * WIDTH, bytes_accessed=12 * DEPTH * ROWS * WIDTH,
            transcendentals=2 * DEPTH * ROWS * WIDTH,
        ),
        name="step",
    )(labels, kappa, inflow)


def solution(mesh):
    return jax.shard_map(
        on_device,
        mesh=mesh,
        in_specs=(P("across", "plane", None), P("across", "plane", None), P("plane", None)),
        out_specs=(P("across", "plane", None), P("plane", "across")),
        check_vma=False,
    )
```

time: 295 us -> 52 us (0.18); the launches traced: 290 us -> 52 us
  waiting for transfers between devices: 162 us -> 0 us
  starting transfers between devices: 48.8 us -> 0 us
  Pallas kernels: 0 us -> 48.7 us
  other arithmetic: 36.9 us -> 0 us
  blocking collectives: 25.4 us -> 0 us
  between operations: 15 us -> 0.64 us
    psum x1 -> x0, waiting for transfers between devices: 152 us -> none  [on_device(): aperture, react = lax.psum((aperture_part, react_part), 'across')]
    ppermute x14 -> x0, starting transfers between devices: 48.8 us -> none  [the longest x7 35.3 us: padded(): lax.ppermute(tail, axis, [(i, (i + 1) % count) for i in range(ends)])]
    pallas_call x0 -> x1, Pallas kernels: none -> 48.7 us  [on_device(): pl.pallas_call(kernel, out_shape=(jax.ShapeDtypeStruct((DEPTH, ROWS, WIDT...]
    psum x1 -> x0, blocking collectives: 25.4 us -> none  [on_device(): flux_total = lax.psum(jnp.sum(flux), 'plane')]
    add x6 -> x0, other arithmetic: 19.9 us -> none  [the longest x1 16.6 us: on_device(): level_new = level + time_step * kappa * flux_norm[None] * slope]
    ppermute x14 -> x0, waiting for transfers between devices: 9.5 us -> none  [the longest x7 5.28 us: padded(): lax.ppermute(head, axis, [((i + 1) % count, i) for i in range(ends)])]
    concatenate x7 -> x0, other arithmetic: 8.41 us -> none  [padded(): jnp.concatenate([lax.ppermute(tail, axis, [(i, (i + 1) % count) for i in...]
    reduce_sum x2 -> x0, other arithmetic: 6.58 us -> none  [the longest x1 5.77 us: column_parts(): aperture_part = jnp.sum(0.5 * (1.0 + tanh_level), axis=0) / depth_total]
  transfers between devices with their start and end apart: 15 -> 0, of which waited for: 4 -> 0; matrix products, arithmetic and copies ran while one was open for 4% -> 0% of each run, Pallas kernels for 0% -> 0%
where the time goes in v1:
time: 52 us
  Pallas kernels  48.7 us (94%)
  local copies, waits for them, and re-layouts  2.63 us (5%)
  between operations  0.64 us (1%)
    pallas_call x1, Pallas kernels, on_device(): pl.pallas_call(kernel, out_shape=(jax.ShapeDtypeStruct((DEPTH, ROWS, WIDT...  48.7 us
    unnamed x2, local copies, waits for them, and re-layouts  2.63 us

profile of v1, /device:TPU:1, one launch (start us, length us, event | category | flops | bytes accessed | tf_op | source)
XLA Modules:
  0.0 52.0 jit_solution(2663010955598124580)
XLA Ops:
  0.6 48.7 %step.1 = (f32[16,64,1024]{2,1,0:T(8,128)S(1)}, f32[64,64]{1,0:T(8,128)S(1)}) custom-call(s32[16,64,1024]{2,1,0:T(8,128)} %labels.1, f32[16,64,1024]{2,1,0:T(8,128)} %kappa.1, f32[64,1024]{1,0:T(8,128)} %inflow.1), custom_call_target="tpu_custom_call" | custom-call | flops 62914560 | bytes 12582912 | tf_op jit(solution)/shard_map/step/pallas_call | solution.py:438
  49.3 2.0 %copy.7 = f32[16,64,1024]{2,1,0:T(8,128)} copy(f32[16,64,1024]{2,1,0:T(8,128)S(1)} %get-tuple-element.4) | data formatting | bytes 8388608
  51.4 0.6 %copy.8 = f32[64,64]{1,0:T(8,128)} copy(f32[64,64]{1,0:T(8,128)S(1)} %get-tuple-element.5) | data formatting | bytes 32768

commit v2 on v1

v2 whole, which is shorter than its diff:
```python
import functools

import jax
import jax.numpy as jnp
from jax import lax
from jax.experimental import pallas as pl
from jax.experimental.pallas import tpu as pltpu
from jax.sharding import PartitionSpec as P

ITERS = 4

front_width = 0.5
time_step = 0.3
leak_rate = 0.05
cheb_low = 0.05
cheb_high = 2.0

MESH = pl.DeviceIdType.MESH
F32 = jnp.float32

DEPTH = 16
ROWS = 64
WIDTH = 1024
GROUP = 16
LINES = 8
BLOCKS = ROWS // LINES
LAST = BLOCKS - 1
HALF = WIDTH // 2
STRIP = 128
PAD = 8
CELLS = float(ROWS * GROUP * WIDTH)
VOXELS = float(DEPTH * GROUP)
TOP_ROW = ROWS * GROUP - 1

EARLY = 2
FIRST = 3


def far_first(c):
    return 4 + (1 - 2 * (c % 2)) * ((c + 1) // 2)


def aligned(index, step):
    return pl.ds(pl.multiple_of(index * step, step), step)


def kernel(
    labels, kappa, inflow, lev, kap, fluxes, scale, press_got,
    lab, flow, part, got, mine, gathered, crossed, relay, rim, rim_got, tile, around, sums, sums_plane, press,
    lab_sem, kap_sem, flow_sem, xs_sem, xr_sem, zs_sem, zr_sem, ds_sem, dr_sem, hs_sem, hr_sem,
    as_sem, ar_sem, ps_sem, pr_sem, fs_sem, fr_sem, ts_sem, tr_sem, ls_sem, lr_sem, rs_sem, rr_sem,
):
    a = lax.axis_index("across")
    p = lax.axis_index("plane")
    z = a // 2
    xh = lax.rem(a, 2)
    other = 1 - xh
    partner = a + other - xh

    def on_across(index):
        return {"plane": p, "across": index}

    def on_plane(index):
        return {"plane": index, "across": a}

    def ring(index, step):
        return lax.rem(index + step + GROUP, GROUP)

    block_id = p * BLOCKS + z
    count = GROUP * BLOCKS
    before = lax.rem(block_id + count - 1, count)
    after = lax.rem(block_id + 1, count)

    def owner(block, side):
        return {"plane": block // BLOCKS, "across": 2 * lax.rem(block, BLOCKS) + side}

    def send(src, dst, send_sem, recv_sem, device):
        return pltpu.make_async_remote_copy(
            src_ref=src, dst_ref=dst, send_sem=send_sem, recv_sem=recv_sem,
            device_id=device, device_id_type=MESH,
        )

    def block_at(c):
        return lax.rem(z + far_first(c), BLOCKS)

    def load_labels(c):
        rows = aligned(block_at(c), LINES)
        return pltpu.make_async_copy(labels.at[:, rows, :], lab.at[:, rows, :], lab_sem.at[c])

    def load_kappa(c):
        rows = aligned(block_at(c), LINES)
        return pltpu.make_async_copy(kappa.at[:, rows, :], kap.at[:, rows, :], kap_sem.at[c])

    @pl.loop(0, BLOCKS)
    def _(c):
        load_labels(c).start()
        load_kappa(c).start()

    my_columns = aligned(xh, HALF)
    load_flow = pltpu.make_async_copy(inflow.at[aligned(z, LINES), my_columns], flow, flow_sem)
    load_flow.start()

    barrier = pltpu.get_barrier_semaphore()

    def greet(device):
        pl.semaphore_signal(barrier, inc=1, device_id=device, device_id_type=MESH)

    for k in range(1, BLOCKS):
        greet(on_across(ring(a, 2 * k)))
    for c in range(FIRST, LAST):
        greet(on_across(2 * block_at(c) + other))
    for block in (before, after):
        for side in (xh, other):
            greet(owner(block, side))
    greet(on_across(partner))

    @pl.loop(1, GROUP)
    def _(k):
        greet(on_plane(ring(p, k)))

    greetings = LAST + (LAST - FIRST) + 4 + 1 + GROUP - 1

    def column_sums(c):
        block = block_at(c)
        rows = aligned(block, LINES)
        load_labels(c).wait()
        load_kappa(c).wait()
        open_sum = jnp.zeros((LINES, WIDTH), F32)
        react_sum = jnp.zeros((LINES, WIDTH), F32)
        for k in range(DEPTH):
            rate = kap[k, rows, :]
            level = jnp.where(lab[k, rows, :] == 0, rate, -rate)
            lev[k + 1, pl.ds(pl.multiple_of(block * LINES + PAD, LINES), LINES), :] = level
            front = jnp.tanh(level * (1.0 / front_width))
            open_sum = open_sum + front
            react_sum = react_sum + rate * (1.0 - front * front)
        for side in range(2):
            part[side, block, 0] = open_sum[:, side * HALF : (side + 1) * HALF]
            part[side, block, 1] = react_sum[:, side * HALF : (side + 1) * HALF]

    def to_partner(c):
        block = block_at(c)
        return send(part.at[other, block], got.at[c], xs_sem.at[c], xr_sem.at[c], on_across(partner))

    def to_owner(c, src):
        return send(src, gathered.at[c], zs_sem.at[c], zr_sem.at[c], on_across(2 * block_at(c) + xh))

    def to_other_owner(c):
        block = block_at(c)
        return send(
            part.at[other, block], crossed.at[c], ds_sem.at[c], dr_sem.at[c], on_across(2 * block + other)
        )

    def pass_on(c):
        if isinstance(c, int) and c == LAST:
            to_partner(c).start()
            return

        @pl.when(c < FIRST)
        def _():
            to_partner(c).start()

        @pl.when(c >= FIRST)
        def _():
            to_other_owner(c).start()
            to_owner(c, part.at[xh, block_at(c)]).start()

    @pl.loop(0, EARLY)
    def _(c):
        column_sums(c)

    pl.semaphore_wait(barrier, greetings)

    @pl.loop(0, EARLY)
    def _(c):
        pass_on(c)

    @pl.loop(EARLY, LAST)
    def _(c):
        column_sums(c)
        pass_on(c)

    column_sums(LAST)
    pass_on(LAST)

    body = pl.ds(PAD, ROWS)
    layer_same = send(
        lev.at[1 + other * (DEPTH - 1), body, :], lev.at[xh * (DEPTH + 1), body, :],
        ls_sem.at[0], lr_sem.at[0], on_across(partner),
    )
    layer_hop = send(
        lev.at[1 + xh * (DEPTH - 1), body, :], relay,
        ls_sem.at[1], lr_sem.at[1], on_across(ring(a, 4 * xh - 2)),
    )
    layer_turn = send(
        relay, lev.at[other * (DEPTH + 1), body, :], ls_sem.at[2], lr_sem.at[2], on_across(partner)
    )
    layers = [layer_same, layer_hop, layer_turn]

    for k in range(DEPTH):
        rim[0, k : k + 1, :] = lev[k + 1, PAD : PAD + 1, :]
        rim[1, k : k + 1, :] = lev[k + 1, PAD + ROWS - 1 : PAD + ROWS, :]
    rims = [
        send(rim.at[0], rim_got.at[1], rs_sem.at[0], rr_sem.at[0], on_plane(ring(p, -1))),
        send(rim.at[1], rim_got.at[0], rs_sem.at[1], rr_sem.at[1], on_plane(ring(p, 1))),
    ]
    for copy in rims:
        copy.start()

    @pl.loop(0, FIRST)
    def _(c):
        to_partner(c).wait_recv()
        mine[c] = part[xh, block_at(c)] + got[c]
        to_owner(c, mine.at[c]).start()

    layer_hop.start()

    to_partner(LAST).wait_recv()
    open_sum = part[xh, z, 0] + got[LAST, 0]
    react_sum = part[xh, z, 1] + got[LAST, 1]
    for c in range(LAST):
        to_owner(c, mine.at[c]).wait_recv()
        open_sum = open_sum + gathered[c, 0]
        react_sum = react_sum + gathered[c, 1]
    for c in range(FIRST, LAST):
        to_other_owner(c).wait_recv()
        open_sum = open_sum + crossed[c, 0]
        react_sum = react_sum + crossed[c, 1]
    aperture = 0.5 + open_sum * (0.5 / VOXELS)
    react = react_sum * (1.0 / (2 * front_width * VOXELS))
    load_flow.wait()
    row = (block_id * LINES + lax.broadcasted_iota(jnp.int32, (LINES, HALF), 0)).astype(F32)
    tile[0] = aperture * aperture * aperture + 0.05
    tile[1] = (1.0 + 2.0 * row / TOP_ROW) * flow[...] + react

    def to_around(line, device, k):
        return send(
            tile, around.at[:, pl.ds(line * LINES, LINES), my_columns], hs_sem.at[k], hr_sem.at[k], device
        )

    tiles = [
        to_around(2, owner(before, other), 0),
        to_around(0, owner(after, other), 1),
        to_around(2, owner(before, xh), 2),
        to_around(0, owner(after, xh), 3),
        to_around(1, on_across(partner), 4),
    ]
    for copy in tiles:
        copy.start()
    around[:, LINES : 2 * LINES, my_columns] = tile[...]
    layer_same.start()

    for copy in rims:
        copy.wait_recv()
    for k in range(DEPTH):
        lev[k + 1, PAD - 1 : PAD, :] = jnp.where(p == 0, 0.0, rim_got[0, k : k + 1, :])
        lev[k + 1, PAD + ROWS : PAD + ROWS + 1, :] = jnp.where(p == GROUP - 1, 0.0, rim_got[1, k : k + 1, :])

    lane = lax.broadcasted_iota(jnp.int32, (LINES, WIDTH), 1)

    def growth(k):
        for block in range(BLOCKS):
            first = PAD + block * LINES
            here = lev[k + 1, first : first + LINES, :]
            dz = lev[k + 2, first : first + LINES, :] - lev[k, first : first + LINES, :]
            dx = lev[k + 1, first + 1 : first + LINES + 1, :] - lev[k + 1, first - 1 : first + LINES - 1, :]
            right = jnp.where(lane == WIDTH - 1, 0.0, pltpu.roll(here, WIDTH - 1, 1))
            left = jnp.where(lane == 0, 0.0, pltpu.roll(here, 1, 1))
            dy = right - left
            slope = jnp.sqrt(dz * dz + dx * dx + dy * dy + 1.0)
            kap[k, block * LINES : (block + 1) * LINES, :] = (0.5 * time_step) * jnp.abs(here) * slope

    @pl.loop(1, DEPTH - 1)
    def _(k):
        growth(k)

    for copy in tiles:
        copy.wait_recv()

    shape = (3 * LINES, WIDTH)
    row_at = (block_id - 1) * LINES + lax.broadcasted_iota(jnp.int32, shape, 0)
    column_at = lax.broadcasted_iota(jnp.int32, shape, 1)
    within = jnp.logical_and(row_at >= 0, row_at <= TOP_ROW)
    has_up = row_at != 0
    has_down = row_at != TOP_ROW
    has_left = column_at != 0
    has_right = column_at != WIDTH - 1

    def from_up(v):
        return pltpu.roll(v, 1, 0)

    def from_down(v):
        return pltpu.roll(v, 3 * LINES - 1, 0)

    def from_left(v):
        return pltpu.roll(v, 1, 1)

    def from_right(v):
        return pltpu.roll(v, WIDTH - 1, 1)

    sides = ((from_down, has_down), (from_up, has_up), (from_right, has_right), (from_left, has_left))
    conduct = jnp.where(within, around[0], 0.0)
    residue = jnp.where(within, around[1], 0.0)
    diagonal = jnp.full(shape, leak_rate, F32)
    weights = []
    for shift, inside in sides:
        face = 0.5 * (conduct + jnp.where(inside, shift(conduct), 0.0))
        diagonal = diagonal + face
        weights.append(jnp.where(inside, face, 0.0))
    inverse = 1.0 / diagonal
    center = (cheb_high + cheb_low) / 2
    radius = (cheb_high - cheb_low) / 2
    sigma_ratio = center / radius
    rho_prev = 1.0 / sigma_ratio
    pressure = jnp.zeros(shape, F32)
    direction = residue * inverse * (1.0 / center)
    for sweep_index in range(ITERS):
        pressure = pressure + direction
        if sweep_index < ITERS - 1:
            image = diagonal * direction
            for weight, (shift, _) in zip(weights, sides):
                image = image - weight * shift(direction)
            residue = residue - image
            rho_next = 1.0 / (2 * sigma_ratio - rho_prev)
            direction = rho_next * rho_prev * direction + (2 * rho_next / radius) * (residue * inverse)
            rho_prev = rho_next
    grad = []
    for shift, inside in sides:
        grad.append(jnp.where(inside, shift(pressure), 0.0))
    grad_x = 0.5 * (grad[0] - grad[1])
    grad_y = 0.5 * (grad[2] - grad[3])
    flux = (conduct * (grad_x * grad_x + grad_y * grad_y) + 0.05)[LINES : 2 * LINES]
    total = flux[:, 0:STRIP]
    for c in range(1, WIDTH // STRIP):
        total = total + flux[:, c * STRIP : (c + 1) * STRIP]
    sums[0] = total

    def sum_blocks(k):
        return send(sums.at[0], sums.at[k], as_sem.at[k], ar_sem.at[k], on_across(ring(a, 2 * k)))

    def sum_plane(k):
        return send(sums_plane.at[0], sums_plane.at[k], ps_sem.at[k], pr_sem.at[k], on_plane(ring(p, k)))

    def flux_out(k):
        return send(fluxes.at[z], fluxes.at[z], fs_sem.at[k], fr_sem.at[k], on_across(ring(a, 2 * k)))

    def press_out(k):
        return send(
            press.at[lax.rem(z + k, BLOCKS)], press_got.at[z], ts_sem.at[k], tr_sem.at[k],
            on_across(ring(a, 2 * k)),
        )

    @pl.loop(0, LAST)
    def _(c):
        sum_blocks(far_first(c)).start()

    fluxes[z] = flux

    @pl.loop(0, LAST)
    def _(c):
        flux_out(far_first(c)).start()

    layer_hop.wait_recv()
    layer_turn.start()

    for c in range(BLOCKS):
        press[c] = pressure[LINES : 2 * LINES, c * STRIP : (c + 1) * STRIP]
    press_got[z] = press[z]

    @pl.loop(1, BLOCKS)
    def _(k):
        sum_blocks(k).wait_recv()

    total = sums[0]
    for k in range(1, BLOCKS):
        total = total + sums[k]
    sums_plane[0] = total

    @pl.loop(1, GROUP)
    def _(k):
        sum_plane(k).start()

    @pl.loop(1, BLOCKS)
    def _(k):
        press_out(k).start()

    layer_same.wait_recv()
    layer_turn.wait_recv()

    @pl.when(a == GROUP - 1)
    def _():
        lev[DEPTH + 1, PAD : PAD + ROWS, :] = jnp.zeros((ROWS, WIDTH), F32)

    growth(DEPTH - 1)

    @pl.when(a == 0)
    def _():
        lev[0, PAD : PAD + ROWS, :] = jnp.zeros((ROWS, WIDTH), F32)

    growth(0)

    @pl.loop(1, GROUP)
    def _(k):
        sum_plane(k).wait_recv()

    total = sums_plane[0]
    for k in range(1, GROUP):
        total = total + sums_plane[k]
    total = jnp.sum(jnp.sum(total, axis=0, keepdims=True), axis=1, keepdims=True)
    scale[...] = jnp.broadcast_to(CELLS / total, scale.shape)

    @pl.loop(1, BLOCKS)
    def _(k):
        flux_out(k).wait_recv()
        press_out(k).wait_recv()

    @pl.loop(0, FIRST)
    def _(c):
        to_partner(c).wait_send()

    to_partner(LAST).wait_send()

    @pl.loop(0, LAST)
    def _(c):
        to_owner(c, mine.at[c]).wait_send()

    @pl.loop(FIRST, LAST)
    def _(c):
        to_other_owner(c).wait_send()

    for copy in [*rims, *layers, *tiles]:
        copy.wait_send()

    @pl.loop(1, BLOCKS)
    def _(k):
        sum_blocks(k).wait_send()
        flux_out(k).wait_send()
        press_out(k).wait_send()

    @pl.loop(1, GROUP)
    def _(k):
        sum_plane(k).wait_send()


def finish(lev, kap, fluxes, scale, press_got, level_new, pressure, level_at, press_at, level_sem, press_sem):
    xh = lax.rem(lax.axis_index("across"), 2)

    def store(block):
        rows = aligned(block, LINES)
        return pltpu.make_async_copy(level_at.at[:, rows, :], level_new.at[:, rows, :], level_sem.at[block])

    @pl.loop(0, BLOCKS)
    def _(block):
        rows = aligned(block, LINES)
        rows_lev = pl.ds(pl.multiple_of(block * LINES + PAD, LINES), LINES)
        norm = fluxes[block] * scale[0:1, 0:1]
        for k in range(DEPTH):
            level_at[k, rows, :] = lev[k + 1, rows_lev, :] + kap[k, rows, :] * norm
        store(block).start()

    for block in range(BLOCKS):
        piece = press_got[block]
        piece = jnp.where(xh == 1, pltpu.roll(piece, STRIP // 2, 1), piece)
        press_at[block * LINES : (block + 1) * LINES, :] = piece[:, : STRIP // 2]
    store_press = pltpu.make_async_copy(press_at, pressure, press_sem)
    store_press.start()

    @pl.loop(0, BLOCKS)
    def _(block):
        store(block).wait()

    store_press.wait()


def on_device(labels, kappa, inflow):
    vmem = functools.partial(pltpu.VMEM, dtype=F32)
    dma = lambda n: pltpu.SemaphoreType.DMA((n,))
    hbm = pl.BlockSpec(memory_space=pltpu.HBM)
    whole = pl.BlockSpec(memory_space=pltpu.VMEM)
    labels, kappa, inflow = (pltpu.with_memory_space_constraint(x, pltpu.HBM) for x in (labels, kappa, inflow))
    parts = pl.pallas_call(
        kernel,
        out_shape=(
            jax.ShapeDtypeStruct((DEPTH + 2, ROWS + 2 * PAD, WIDTH), F32),
            jax.ShapeDtypeStruct((DEPTH, ROWS, WIDTH), F32),
            jax.ShapeDtypeStruct((BLOCKS, LINES, WIDTH), F32),
            jax.ShapeDtypeStruct((LINES, STRIP), F32),
            jax.ShapeDtypeStruct((BLOCKS, LINES, STRIP), F32),
        ),
        in_specs=[hbm, hbm, hbm],
        out_specs=(whole,) * 5,
        scratch_shapes=[
            pltpu.VMEM((DEPTH, ROWS, WIDTH), jnp.int32),
            vmem((LINES, HALF)),
            vmem((2, BLOCKS, 2, LINES, HALF)),
            vmem((BLOCKS, 2, LINES, HALF)),
            vmem((LAST, 2, LINES, HALF)),
            vmem((LAST, 2, LINES, HALF)),
            vmem((LAST, 2, LINES, HALF)),
            vmem((ROWS, WIDTH)),
            vmem((2, DEPTH, WIDTH)),
            vmem((2, DEPTH, WIDTH)),
            vmem((2, LINES, HALF)),
            vmem((2, 3 * LINES, WIDTH)),
            vmem((BLOCKS, LINES, STRIP)),
            vmem((GROUP, LINES, STRIP)),
            vmem((BLOCKS, LINES, STRIP)),
            dma(BLOCKS), dma(BLOCKS), pltpu.SemaphoreType.DMA,
            dma(BLOCKS), dma(BLOCKS),
            dma(BLOCKS), dma(BLOCKS), dma(BLOCKS), dma(BLOCKS),
            dma(5), dma(5),
            dma(BLOCKS), dma(BLOCKS), dma(GROUP), dma(GROUP),
            dma(BLOCKS), dma(BLOCKS), dma(BLOCKS), dma(BLOCKS),
            dma(3), dma(3), dma(2), dma(2),
        ],
        compiler_params=pltpu.CompilerParams(
            collective_id=0, has_side_effects=True, vmem_limit_bytes=32 * 2**20
        ),
        cost_estimate=pl.CostEstimate(
            flops=60 * DEPTH * ROWS * WIDTH, bytes_accessed=8 * DEPTH * ROWS * WIDTH,
            transcendentals=2 * DEPTH * ROWS * WIDTH,
        ),
        name="step",
    )(labels, kappa, inflow)
    return pl.pallas_call(
        finish,
        out_shape=(
            jax.ShapeDtypeStruct((DEPTH, ROWS, WIDTH), F32),
            jax.ShapeDtypeStruct((ROWS, STRIP // 2), F32),
        ),
        in_specs=[whole] * 5,
        out_specs=(hbm, hbm),
        scratch_shapes=[
            vmem((DEPTH, ROWS, WIDTH)),
            vmem((ROWS, STRIP // 2)),
            dma(BLOCKS),
            pltpu.SemaphoreType.DMA,
        ],
        compiler_params=pltpu.CompilerParams(vmem_limit_bytes=16 * 2**20),
        cost_estimate=pl.CostEstimate(
            flops=2 * DEPTH * ROWS * WIDTH, bytes_accessed=4 * DEPTH * ROWS * WIDTH, transcendentals=0
        ),
        name="finish",
    )(*parts)


def solution(mesh):
    return jax.shard_map(
        on_device,
        mesh=mesh,
        in_specs=(P("across", "plane", None), P("across", "plane", None), P("plane", None)),
        out_specs=(P("across", "plane", None), P("plane", "across")),
        check_vma=False,
    )
```

time: 52 us -> 43.6 us (0.84)
  Pallas kernels: 48.7 us -> 42.9 us
  local copies, waits for them, and re-layouts: 2.63 us -> 0 us
    pallas_call x1 -> x2, Pallas kernels: 48.7 us -> 42.9 us  [the longest x1 40.7 us: on_device(): pl.pallas_call(kernel, out_shape=(jax.ShapeDtypeStruct((DEPTH + 2, ROWS +...]
    unnamed x2 -> x0, local copies, waits for them, and re-layouts: 2.63 us -> none
where the time goes in v2:
time: 43.6 us; the launch traced here: 43.5 us
  Pallas kernels  42.9 us (98%)
  between operations  0.64 us (1%)
    pallas_call x1, Pallas kernels, on_device(): pl.pallas_call(kernel, out_shape=(jax.ShapeDtypeStruct((DEPTH + 2, ROWS +...  40.7 us
    pallas_call x1, Pallas kernels, on_device(): pl.pallas_call(finish, out_shape=(jax.ShapeDtypeStruct((DEPTH, ROWS, WIDT...  2.17 us

profile of v2, /device:TPU:1, one launch (start us, length us, event | category | flops | bytes accessed | tf_op | source)
XLA Modules:
  0.0 43.5 jit_solution(17340798521706256661)
XLA Ops:
  0.6 40.7 %step.1 = (f32[18,80,1024]{2,1,0:T(8,128)S(1)}, f32[16,64,1024]{2,1,0:T(8,128)S(1)}, f32[8,8,1024]{2,1,0:T(8,128)S(1)}, f32[8,128]{1,0:T(8,128)S(1)}, f32[8,8,128]{2,1,0:T(8,128)S(1)}) custom-call(s32[16,64,1024]{2,1,0:T(8,128)} %labels.1, f32[16,64,1024]{2,1,0:T(8,128)} %kappa.1, f32[64,1024]{1,0:T(8,128)} %inflow.1), custom_call_target="tpu_custom_call" | custom-call | flops 62914560 | bytes 8388608 | tf_op jit(solution)/shard_map/step/pallas_call | solution.py:481
  41.3 2.2 %finish.1 = (f32[16,64,1024]{2,1,0:T(8,128)}, f32[64,64]{1,0:T(8,128)}) custom-call(f32[18,80,1024]{2,1,0:T(8,128)S(1)} %get-tuple-element.7.lev, f32[16,64,1024]{2,1,0:T(8,128)S(1)} %get-tuple-element.8.kap, f32[8,8,1024]{2,1,0:T(8,128)S(1)} %get-tuple-element.9.fluxes, f32[8,128]{1,0:T(8,128)S(1)} %get-tuple-element.10.scale, ...), custom_call_target="tpu_custom_call" | custom-call | flops 2097152 | bytes 4194304 | tf_op jit(solution)/shard_map/finish/pallas_call | solution.py:525

commit v3 on v2

--- a/solution.py
+++ b/solution.py
@@ -32,8 +32,19 @@
 VOXELS = float(DEPTH * GROUP)
 TOP_ROW = ROWS * GROUP - 1
 
-EARLY = 2
-FIRST = 3
+EARLY = (8, 8, 8, 4, 1, 1, 1, 1)
+ORDER = (4, 2, 3, 6, 5, 1, 7, 0)
+VIA = (0, 2, 4)
+STRAIGHT = (1, 3, 5, 6)
+
+
+def pick(table, c):
+    if isinstance(c, int):
+        return table[c]
+    value = table[0]
+    for index in range(1, len(table)):
+        value = jnp.where(c == index, table[index], value)
+    return value
 
 
 def far_first(c):
@@ -81,7 +92,7 @@
         )
 
     def block_at(c):
-        return lax.rem(z + far_first(c), BLOCKS)
+        return lax.rem(z + pick(ORDER, c), BLOCKS)
 
     def load_labels(c):
         rows = aligned(block_at(c), LINES)
@@ -107,7 +118,7 @@
 
     for k in range(1, BLOCKS):
         greet(on_across(ring(a, 2 * k)))
-    for c in range(FIRST, LAST):
+    for c in STRAIGHT:
         greet(on_across(2 * block_at(c) + other))
     for block in (before, after):
         for side in (xh, other):
@@ -118,7 +129,7 @@
     def _(k):
         greet(on_plane(ring(p, k)))
 
-    greetings = LAST + (LAST - FIRST) + 4 + 1 + GROUP - 1
+    greetings = LAST + len(STRAIGHT) + 4 + 1 + GROUP - 1
 
     def column_sums(c):
         block = block_at(c)
@@ -152,36 +163,33 @@
         )
 
     def pass_on(c):
-        if isinstance(c, int) and c == LAST:
-            to_partner(c).start()
-            return
-
-        @pl.when(c < FIRST)
+        via = pick(tuple(int(k in VIA or k == LAST) for k in range(BLOCKS)), c) == 1
+
+        @pl.when(via)
         def _():
             to_partner(c).start()
 
-        @pl.when(c >= FIRST)
+        @pl.when(jnp.logical_not(via))
         def _():
+            to_owner(c, part.at[xh, block_at(c)]).start()
             to_other_owner(c).start()
-            to_owner(c, part.at[xh, block_at(c)]).start()
-
-    @pl.loop(0, EARLY)
+
+    early = pick(EARLY, z)
+
+    @pl.loop(0, early)
     def _(c):
         column_sums(c)
 
     pl.semaphore_wait(barrier, greetings)
 
-    @pl.loop(0, EARLY)
+    @pl.loop(0, early)
     def _(c):
         pass_on(c)
 
-    @pl.loop(EARLY, LAST)
+    @pl.loop(early, BLOCKS)
     def _(c):
         column_sums(c)
         pass_on(c)
-
-    column_sums(LAST)
-    pass_on(LAST)
 
     body = pl.ds(PAD, ROWS)
     layer_same = send(
@@ -207,8 +215,9 @@
     for copy in rims:
         copy.start()
 
-    @pl.loop(0, FIRST)
-    def _(c):
+    @pl.loop(0, len(VIA))
+    def _(k):
+        c = pick(VIA, k)
         to_partner(c).wait_recv()
         mine[c] = part[xh, block_at(c)] + got[c]
         to_owner(c, mine.at[c]).start()
@@ -222,7 +231,7 @@
         to_owner(c, mine.at[c]).wait_recv()
         open_sum = open_sum + gathered[c, 0]
         react_sum = react_sum + gathered[c, 1]
-    for c in range(FIRST, LAST):
+    for c in STRAIGHT:
         to_other_owner(c).wait_recv()
         open_sum = open_sum + crossed[c, 0]
         react_sum = react_sum + crossed[c, 1]
@@ -333,7 +342,7 @@
     total = flux[:, 0:STRIP]
     for c in range(1, WIDTH // STRIP):
         total = total + flux[:, c * STRIP : (c + 1) * STRIP]
-    sums[0] = total
+    sums[0] = jnp.sum(total, axis=0, keepdims=True)
 
     def sum_blocks(k):
         return send(sums.at[0], sums.at[k], as_sem.at[k], ar_sem.at[k], on_across(ring(a, 2 * k)))
@@ -356,9 +365,11 @@
 
     fluxes[z] = flux
 
-    @pl.loop(0, LAST)
-    def _(c):
-        flux_out(far_first(c)).start()
+    @pl.loop(0, BLOCKS)
+    def _(reached):
+        @pl.when(reached != z)
+        def _():
+            flux_out(lax.rem(reached - z + BLOCKS, BLOCKS)).start()
 
     layer_hop.wait_recv()
     layer_turn.start()
@@ -406,7 +417,7 @@
     total = sums_plane[0]
     for k in range(1, GROUP):
         total = total + sums_plane[k]
-    total = jnp.sum(jnp.sum(total, axis=0, keepdims=True), axis=1, keepdims=True)
+    total = jnp.sum(total, axis=1, keepdims=True)
     scale[...] = jnp.broadcast_to(CELLS / total, scale.shape)
 
     @pl.loop(1, BLOCKS)
@@ -414,9 +425,9 @@
         flux_out(k).wait_recv()
         press_out(k).wait_recv()
 
-    @pl.loop(0, FIRST)
-    def _(c):
-        to_partner(c).wait_send()
+    @pl.loop(0, len(VIA))
+    def _(k):
+        to_partner(pick(VIA, k)).wait_send()
 
     to_partner(LAST).wait_send()
 
@@ -424,8 +435,7 @@
     def _(c):
         to_owner(c, mine.at[c]).wait_send()
 
-    @pl.loop(FIRST, LAST)
-    def _(c):
+    for c in STRAIGHT:
         to_other_owner(c).wait_send()
 
     for copy in [*rims, *layers, *tiles]:
@@ -502,8 +512,8 @@
             vmem((2, DEPTH, WIDTH)),
             vmem((2, LINES, HALF)),
             vmem((2, 3 * LINES, WIDTH)),
-            vmem((BLOCKS, LINES, STRIP)),
-            vmem((GROUP, LINES, STRIP)),
+            vmem((BLOCKS, 1, STRIP)),
+            vmem((GROUP, 1, STRIP)),
             vmem((BLOCKS, LINES, STRIP)),
             dma(BLOCKS), dma(BLOCKS), pltpu.SemaphoreType.DMA,
             dma(BLOCKS), dma(BLOCKS),

time: 43.6 us -> 42.4 us (0.972)
  Pallas kernels: 42.9 us -> 41.7 us
    pallas_call x1, Pallas kernels: 40.7 us -> 39.5 us  [on_device(): pl.pallas_call(kernel, out_shape=(jax.ShapeDtypeStruct((DEPTH + 2, ROWS +...]
where the time goes in v3:
time: 42.4 us; the launch traced here: 42.3 us
  Pallas kernels  41.7 us (98%)
  between operations  0.64 us (2%)
    pallas_call x1, Pallas kernels, on_device(): pl.pallas_call(kernel, out_shape=(jax.ShapeDtypeStruct((DEPTH + 2, ROWS +...  39.5 us
    pallas_call x1, Pallas kernels, on_device(): pl.pallas_call(finish, out_shape=(jax.ShapeDtypeStruct((DEPTH, ROWS, WIDT...  2.17 us

profile of v3, /device:TPU:1, one launch (start us, length us, event | category | flops | bytes accessed | tf_op | source)
XLA Modules:
  0.0 42.3 jit_solution(10715513197216153322)
XLA Ops:
  0.6 39.5 %step.1 = (f32[18,80,1024]{2,1,0:T(8,128)S(1)}, f32[16,64,1024]{2,1,0:T(8,128)S(1)}, f32[8,8,1024]{2,1,0:T(8,128)S(1)}, f32[8,128]{1,0:T(8,128)S(1)}, f32[8,8,128]{2,1,0:T(8,128)S(1)}) custom-call(s32[16,64,1024]{2,1,0:T(8,128)} %labels.1, f32[16,64,1024]{2,1,0:T(8,128)} %kappa.1, f32[64,1024]{1,0:T(8,128)} %inflow.1), custom_call_target="tpu_custom_call" | custom-call | flops 62914560 | bytes 8388608 | tf_op jit(solution)/shard_map/step/pallas_call | solution.py:491
  40.1 2.2 %finish.1 = (f32[16,64,1024]{2,1,0:T(8,128)}, f32[64,64]{1,0:T(8,128)}) custom-call(f32[18,80,1024]{2,1,0:T(8,128)S(1)} %get-tuple-element.7.lev, f32[16,64,1024]{2,1,0:T(8,128)S(1)} %get-tuple-element.8.kap, f32[8,8,1024]{2,1,0:T(8,128)S(1)} %get-tuple-element.9.fluxes, f32[8,128]{1,0:T(8,128)S(1)} %get-tuple-element.10.scale, ...), custom_call_target="tpu_custom_call" | custom-call | flops 2097152 | bytes 4194304 | tf_op jit(solution)/shard_map/finish/pallas_call | solution.py:535

commit v4 on v3

--- a/solution.py
+++ b/solution.py
@@ -102,21 +102,19 @@
         rows = aligned(block_at(c), LINES)
         return pltpu.make_async_copy(kappa.at[:, rows, :], kap.at[:, rows, :], kap_sem.at[c])
 
-    @pl.loop(0, BLOCKS)
+    @pl.loop(0, 2)
     def _(c):
         load_labels(c).start()
         load_kappa(c).start()
 
     my_columns = aligned(xh, HALF)
     load_flow = pltpu.make_async_copy(inflow.at[aligned(z, LINES), my_columns], flow, flow_sem)
-    load_flow.start()
-
     barrier = pltpu.get_barrier_semaphore()
 
     def greet(device):
         pl.semaphore_signal(barrier, inc=1, device_id=device, device_id_type=MESH)
 
-    for k in range(1, BLOCKS):
+    for k in (4, 3, 5, 2, 6, 1, 7):
         greet(on_across(ring(a, 2 * k)))
     for c in STRAIGHT:
         greet(on_across(2 * block_at(c) + other))
@@ -128,6 +126,13 @@
     @pl.loop(1, GROUP)
     def _(k):
         greet(on_plane(ring(p, k)))
+
+    @pl.loop(2, BLOCKS)
+    def _(c):
+        load_labels(c).start()
+        load_kappa(c).start()
+
+    load_flow.start()
 
     greetings = LAST + len(STRAIGHT) + 4 + 1 + GROUP - 1
 
@@ -410,6 +415,32 @@
 
     growth(0)
 
+    @pl.loop(0, len(VIA))
+    def _(k):
+        to_partner(pick(VIA, k)).wait_send()
+
+    to_partner(LAST).wait_send()
+
+    @pl.loop(0, LAST)
+    def _(c):
+        to_owner(c, mine.at[c]).wait_send()
+
+    for c in STRAIGHT:
+        to_other_owner(c).wait_send()
+
+    for copy in [*rims, *layers, *tiles]:
+        copy.wait_send()
+
+    @pl.loop(1, BLOCKS)
+    def _(k):
+        sum_blocks(k).wait_send()
+        flux_out(k).wait_send()
+        press_out(k).wait_send()
+
+    @pl.loop(1, GROUP)
+    def _(k):
+        sum_plane(k).wait_send()
+
     @pl.loop(1, GROUP)
     def _(k):
         sum_plane(k).wait_recv()
@@ -424,32 +455,6 @@
     def _(k):
         flux_out(k).wait_recv()
         press_out(k).wait_recv()
-
-    @pl.loop(0, len(VIA))
-    def _(k):
-        to_partner(pick(VIA, k)).wait_send()
-
-    to_partner(LAST).wait_send()
-
-    @pl.loop(0, LAST)
-    def _(c):
-        to_owner(c, mine.at[c]).wait_send()
-
-    for c in STRAIGHT:
-        to_other_owner(c).wait_send()
-
-    for copy in [*rims, *layers, *tiles]:
-        copy.wait_send()
-
-    @pl.loop(1, BLOCKS)
-    def _(k):
-        sum_blocks(k).wait_send()
-        flux_out(k).wait_send()
-        press_out(k).wait_send()
-
-    @pl.loop(1, GROUP)
-    def _(k):
-        sum_plane(k).wait_send()
 
 
 def finish(lev, kap, fluxes, scale, press_got, level_new, pressure, level_at, press_at, level_sem, press_sem):

time: 42.4 us -> 42.3 us (level)
  no operation moved by 1% of the time
where the time goes in v4:
time: 42.3 us; the launch traced here: 42.2 us
  Pallas kernels  41.6 us (98%)
  between operations  0.64 us (2%)
    pallas_call x1, Pallas kernels, on_device(): pl.pallas_call(kernel, out_shape=(jax.ShapeDtypeStruct((DEPTH + 2, ROWS +...  39.4 us
    pallas_call x1, Pallas kernels, on_device(): pl.pallas_call(finish, out_shape=(jax.ShapeDtypeStruct((DEPTH, ROWS, WIDT...  2.17 us

profile of v4, /device:TPU:1, one launch (start us, length us, event | category | flops | bytes accessed | tf_op | source)
XLA Modules:
  0.0 42.2 jit_solution(17759369390515768119)
XLA Ops:
  0.6 39.4 %step.1 = (f32[18,80,1024]{2,1,0:T(8,128)S(1)}, f32[16,64,1024]{2,1,0:T(8,128)S(1)}, f32[8,8,1024]{2,1,0:T(8,128)S(1)}, f32[8,128]{1,0:T(8,128)S(1)}, f32[8,8,128]{2,1,0:T(8,128)S(1)}) custom-call(s32[16,64,1024]{2,1,0:T(8,128)} %labels.1, f32[16,64,1024]{2,1,0:T(8,128)} %kappa.1, f32[64,1024]{1,0:T(8,128)} %inflow.1), custom_call_target="tpu_custom_call" | custom-call | flops 62914560 | bytes 8388608 | tf_op jit(solution)/shard_map/step/pallas_call | solution.py:496
  40.0 2.2 %finish.1 = (f32[16,64,1024]{2,1,0:T(8,128)}, f32[64,64]{1,0:T(8,128)}) custom-call(f32[18,80,1024]{2,1,0:T(8,128)S(1)} %get-tuple-element.7.lev, f32[16,64,1024]{2,1,0:T(8,128)S(1)} %get-tuple-element.8.kap, f32[8,8,1024]{2,1,0:T(8,128)S(1)} %get-tuple-element.9.fluxes, f32[8,128]{1,0:T(8,128)S(1)} %get-tuple-element.10.scale, ...), custom_call_target="tpu_custom_call" | custom-call | flops 2097152 | bytes 4194304 | tf_op jit(solution)/shard_map/finish/pallas_call | solution.py:540

commit v5 on v3

--- a/solution.py
+++ b/solution.py
@@ -203,7 +203,8 @@
     layer_turn = send(
         relay, lev.at[other * (DEPTH + 1), body, :], ls_sem.at[2], lr_sem.at[2], on_across(partner)
     )
-    layers = [layer_same, layer_hop, layer_turn]
+    has_both = jnp.logical_and(a != 0, a != GROUP - 1)
+    partner_has_both = jnp.logical_and(partner != 0, partner != GROUP - 1)
 
     for k in range(DEPTH):
         rim[0, k : k + 1, :] = lev[k + 1, PAD : PAD + 1, :]
@@ -222,7 +223,12 @@
         mine[c] = part[xh, block_at(c)] + got[c]
         to_owner(c, mine.at[c]).start()
 
-    layer_hop.start()
+    layer_same.start()
+
+    @pl.when(has_both)
+    def _():
+        layer_hop.start()
+
 
     to_partner(LAST).wait_recv()
     open_sum = part[xh, z, 0] + got[LAST, 0]
@@ -257,7 +263,6 @@
     for copy in tiles:
         copy.start()
     around[:, LINES : 2 * LINES, my_columns] = tile[...]
-    layer_same.start()
 
     for copy in rims:
         copy.wait_recv()
@@ -371,8 +376,11 @@
         def _():
             flux_out(lax.rem(reached - z + BLOCKS, BLOCKS)).start()
 
-    layer_hop.wait_recv()
-    layer_turn.start()
+    @pl.when(partner_has_both)
+    def _():
+        layer_hop.wait_recv()
+        layer_turn.start()
+
 
     for c in range(BLOCKS):
         press[c] = pressure[LINES : 2 * LINES, c * STRIP : (c + 1) * STRIP]
@@ -396,7 +404,11 @@
         press_out(k).start()
 
     layer_same.wait_recv()
-    layer_turn.wait_recv()
+
+    @pl.when(has_both)
+    def _():
+        layer_turn.wait_recv()
+
 
     @pl.when(a == GROUP - 1)
     def _():
@@ -438,8 +450,16 @@
     for c in STRAIGHT:
         to_other_owner(c).wait_send()
 
-    for copy in [*rims, *layers, *tiles]:
+    for copy in [*rims, layer_same, *tiles]:
         copy.wait_send()
+
+    @pl.when(has_both)
+    def _():
+        layer_hop.wait_send()
+
+    @pl.when(partner_has_both)
+    def _():
+        layer_turn.wait_send()
 
     @pl.loop(1, BLOCKS)
     def _(k):

time: 42.4 us -> 42.5 us (level)
  no operation moved by 1% of the time
where the time goes in v5:
time: 42.5 us; the launch traced here: 42.4 us
  Pallas kernels  41.8 us (98%)
  between operations  0.64 us (2%)
    pallas_call x1, Pallas kernels, on_device(): pl.pallas_call(kernel, out_shape=(jax.ShapeDtypeStruct((DEPTH + 2, ROWS +...  39.6 us
    pallas_call x1, Pallas kernels, on_device(): pl.pallas_call(finish, out_shape=(jax.ShapeDtypeStruct((DEPTH, ROWS, WIDT...  2.17 us

profile of v5, /device:TPU:1, one launch (start us, length us, event | category | flops | bytes accessed | tf_op | source)
XLA Modules:
  0.0 42.4 jit_solution(419801977186753014)
XLA Ops:
  0.6 39.6 %step.1 = (f32[18,80,1024]{2,1,0:T(8,128)S(1)}, f32[16,64,1024]{2,1,0:T(8,128)S(1)}, f32[8,8,1024]{2,1,0:T(8,128)S(1)}, f32[8,128]{1,0:T(8,128)S(1)}, f32[8,8,128]{2,1,0:T(8,128)S(1)}) custom-call(s32[16,64,1024]{2,1,0:T(8,128)} %labels.1, f32[16,64,1024]{2,1,0:T(8,128)} %kappa.1, f32[64,1024]{1,0:T(8,128)} %inflow.1), custom_call_target="tpu_custom_call" | custom-call | flops 62914560 | bytes 8388608 | tf_op jit(solution)/shard_map/step/pallas_call | solution.py:511
  40.3 2.2 %finish.1 = (f32[16,64,1024]{2,1,0:T(8,128)}, f32[64,64]{1,0:T(8,128)}) custom-call(f32[18,80,1024]{2,1,0:T(8,128)S(1)} %get-tuple-element.7.lev, f32[16,64,1024]{2,1,0:T(8,128)S(1)} %get-tuple-element.8.kap, f32[8,8,1024]{2,1,0:T(8,128)S(1)} %get-tuple-element.9.fluxes, f32[8,128]{1,0:T(8,128)S(1)} %get-tuple-element.10.scale, ...), custom_call_target="tpu_custom_call" | custom-call | flops 2097152 | bytes 4194304 | tf_op jit(solution)/shard_map/finish/pallas_call | solution.py:555
